TPU v7x, 128 devices: a whole 4x4x4 slice. The times are simulated.
128 devices in a mesh: req: 8 (over x, core), exp: 16 (over y, z).
Axes of the slice: x: 4, y: 4, z: 4, core: 2. Of those that a mesh axis runs over, the one named last changes fastest.
Arguments:
- tokens: bfloat16 [8320, 2048], P('req'), may hold values from -6 to 6
- attn_gain: bfloat16 [2048], replicated, may hold values from 0.099609375 to 1.8984375
- wq_nope: bfloat16 [2048, 2048], P(None, 'exp'), may hold values from -0.125 to 0.125
- wq_rope: bfloat16 [2048, 1024], P(None, 'exp'), may hold values from -0.125 to 0.125
- w_latent: bfloat16 [2048, 512], replicated, may hold values from -0.125 to 0.125
- w_krope: bfloat16 [2048, 64], replicated, may hold values from -0.125 to 0.125
- latent_gain: bfloat16 [512], replicated, may hold values from 0.099609375 to 1.8984375
- w_uk: bfloat16 [512, 2048], P(None, 'exp'), may hold values from -0.25 to 0.25
- w_uv: bfloat16 [512, 2048], P(None, 'exp'), may hold values from -0.25 to 0.25
- w_out: bfloat16 [2048, 2048], P('exp'), may hold values from -0.125 to 0.125
- moe_gain: bfloat16 [2048], replicated, may hold values from 0.099609375 to 1.8984375
- w_router: bfloat16 [2048, 64], replicated, may hold values from -0.125 to 0.125
- w_gate: bfloat16 [128, 2048, 704], P(('req', 'exp')), may hold values from -0.125 to 0.125
- w_up: bfloat16 [128, 2048, 704], P(('req', 'exp')), may hold values from -0.125 to 0.125
- w_down: bfloat16 [128, 704, 2048], P(('req', 'exp')), may hold values from -0.15625 to 0.15625
- routes: int32 [8320, 6], P(('req', 'exp')), may hold values from 0 to 63, all different within a row; in each aligned block of 65 rows (0 to 64, 65 to 129, ...) at most 10 rows name the same one
- cache_latent: bfloat16 [128, 16, 32, 512], P('req', 'exp'), may hold values from -300 to 300
- cache_rope: bfloat16 [128, 16, 2048], P('req', 'exp'), may hold values from -6 to 6
- mig_dest: int32 [128], P('req'), may hold values from 0 to 7, as said below
- page_table: int32 [128, 16], P('req'), may hold values from 0 to 15, each once within a row
- cache_len: int32 [128], P('req'), may hold values from 1 to 512
- span_slot: int32 [8], P('req'), may hold values from 0 to 15
Outputs:
- mixed: bfloat16 [8320, 2048], P(('req', 'exp'))
Inputs may be any that keep to these rules, and one draw needn't show every extreme that they name: `routes`: among the rows of one device, no expert is named by more than 10 rows, a bound that some block reaches. `mig_dest`: among the 16 slots of each group, exactly 2 go to each group, itself included.
All inputs are finite; a program needn't handle non-finite values.
Results may differ from a plain program's by a relative error of at most 0.019.
The roundings to bfloat16 on the way count: a program that leaves them out, or rounds other values in their place, can miss the bound.
Values may be sent and summed in bfloat16 or wider, within the bound.
No kernel may reach another device: no remote copies, remote signals or barrier semaphores. Data moves between devices by JAX's collectives and lax.ppermute only.
A program may use at most 128 MiB of HBM per device.

v0:
```python
import math
import jax
import jax.numpy as jnp
from jax import lax
from jax.sharding import PartitionSpec as P

DN = 128
DR = 64
TOP = 6
SPAN = 1024
theta_base = 50000.0
route_scale = 2.446
norm_eps = 1e-06


def rms_scale(values, gain_values):
    widened = values.astype(jnp.float32)
    mean_square = jnp.mean(widened * widened, axis=-1, keepdims=True)
    return widened * lax.rsqrt(mean_square + norm_eps) * gain_values.astype(jnp.float32)


def rope_angles(positions, rope_width):
    exponent = jnp.arange(rope_width // 2, dtype=jnp.float32) * (2.0 / rope_width)
    frequency = jnp.exp(-exponent * math.log(theta_base))
    return positions.astype(jnp.float32)[:, None] * frequency[None, :]


def rotate(values, angles):
    half_width = values.shape[-1] // 2
    cosine = jnp.cos(angles)
    sine_part = jnp.sin(angles)
    first_half = values[..., :half_width]
    second_half = values[..., half_width:]
    return jnp.concatenate(
        [
            first_half * cosine - second_half * sine_part,
            second_half * cosine + first_half * sine_part,
        ],
        axis=-1,
    )


def group_positions(lengths, span_slots, span_width):
    starts = jnp.take(lengths, span_slots)
    span_positions = starts[:, None] + jnp.arange(span_width, dtype=jnp.int32)[None, :]
    return jnp.concatenate([span_positions.reshape(-1), lengths])


def dot_transposed(left_side, right_side):
    return lax.dot_general(
        left_side, right_side, (((1,), (1,)), ((), ())), preferred_element_type=jnp.float32
    )


def soft_weights(scores, visible):
    masked = jnp.where(visible, scores, -jnp.inf)
    row_top = jnp.max(masked, axis=-1, keepdims=True)
    raised = jnp.where(visible, jnp.exp(masked - row_top), 0.0)
    return (raised / jnp.sum(raised, axis=-1, keepdims=True)).astype(jnp.bfloat16)


def attend_head(
    query_latent,
    query_rope,
    new_latent,
    new_rope,
    cache_keys,
    cache_rope_keys,
    lengths,
    span_slots,
    span_width,
    scale_factor,
):
    cache_size = cache_keys.shape[1]
    key_index = jnp.arange(cache_size + span_width, dtype=jnp.int32)
    row_index = jnp.arange(span_width, dtype=jnp.int32)
    results = []
    request = span_slots[0]
    keys_latent = jnp.concatenate([cache_keys[request], new_latent[0:span_width]], axis=0)
    keys_rope = jnp.concatenate([cache_rope_keys[request], new_rope[0:span_width]], axis=0)
    scores = (
        dot_transposed(query_latent[0:span_width], keys_latent)
        + dot_transposed(query_rope[0:span_width], keys_rope)
    ) * scale_factor
    visible = jnp.where(
        key_index[None, :] < cache_size,
        key_index[None, :] < lengths[request],
        key_index[None, :] - cache_size <= row_index[:, None],
    )
    weights = soft_weights(scores, visible)
    results.append(
        jnp.dot(weights, keys_latent, preferred_element_type=jnp.float32).astype(jnp.bfloat16)
    )
    dec_start = span_slots.shape[0] * span_width
    dec_latent = query_latent[dec_start:]
    dec_rope = query_rope[dec_start:]
    own_latent = new_latent[dec_start:]
    own_rope = new_rope[dec_start:]
    cache_scores = (
        jnp.einsum("jr,jpr->jp", dec_latent, cache_keys, preferred_element_type=jnp.float32)
        + jnp.einsum("je,jpe->jp", dec_rope, cache_rope_keys, preferred_element_type=jnp.float32)
    ) * scale_factor
    self_scores = (
        jnp.sum(dec_latent.astype(jnp.float32) * own_latent.astype(jnp.float32), axis=1)
        + jnp.sum(dec_rope.astype(jnp.float32) * own_rope.astype(jnp.float32), axis=1)
    ) * scale_factor
    seen = jnp.arange(cache_size, dtype=jnp.int32)[None, :] < lengths[:, None]
    masked = jnp.where(seen, cache_scores, -jnp.inf)
    row_top = jnp.maximum(jnp.max(masked, axis=1), self_scores)
    cache_raised = jnp.where(seen, jnp.exp(masked - row_top[:, None]), 0.0)
    self_raised = jnp.exp(self_scores - row_top)
    totals = jnp.sum(cache_raised, axis=1) + self_raised
    cache_weights = (cache_raised / totals[:, None]).astype(jnp.bfloat16)
    self_weights = (self_raised / totals).astype(jnp.bfloat16)
    dec_out = jnp.einsum(
        "jp,jpr->jr", cache_weights, cache_keys, preferred_element_type=jnp.float32
    ) + self_weights.astype(jnp.float32)[:, None] * own_latent.astype(jnp.float32)
    results.append(dec_out.astype(jnp.bfloat16))
    return jnp.concatenate(results, axis=0)


def one_half(inputs, gate_part, up_part, down_part):
    hidden = (
        jax.nn.silu(jnp.dot(inputs, gate_part, preferred_element_type=jnp.float32))
        * jnp.dot(inputs, up_part, preferred_element_type=jnp.float32)
    ).astype(jnp.bfloat16)
    return jnp.dot(hidden, down_part, preferred_element_type=jnp.float32).astype(jnp.bfloat16)


def expert_halves(received, w_gate, w_up, w_down):
    sources, halves, slot_count, model_width = received.shape
    inputs = received[:, 0].reshape(sources * slot_count, model_width)
    output = one_half(inputs, w_gate[0], w_up[0], w_down[0])
    results = [output.reshape(sources, slot_count, model_width)]
    return jnp.stack(results, axis=1)


def shards(
    tokens,
    attn_gain,
    wq_nope,
    wq_rope,
    w_latent,
    w_krope,
    latent_gain,
    w_uk,
    w_uv,
    w_out,
    moe_gain,
    w_router,
    w_gate,
    w_up,
    w_down,
    routes,
    cache_latent,
    cache_rope,
    mig_dest,
    page_table,
    cache_len,
    span_slot,
):
    req_count = lax.axis_size("req")
    exp_count = lax.axis_size("exp")
    device_count = req_count * exp_count
    req_group = mig_dest.shape[0]
    move_count = req_group // req_count
    rows_group = tokens.shape[0]
    rows_device = rows_group // exp_count
    model_width = tokens.shape[1]
    heads_device = wq_nope.shape[1] // DN
    scale_factor = 1.0 / math.sqrt(DN + DR)
    slot_ids = jnp.arange(req_group, dtype=jnp.int32)
    earlier = (mig_dest[None, :] == mig_dest[:, None]) & (slot_ids[None, :] < slot_ids[:, None])
    placed = mig_dest * move_count + jnp.sum(earlier.astype(jnp.int32), axis=1)
    source_slot = jnp.argmax((placed[None, :] == slot_ids[:, None]).astype(jnp.int32), axis=1)
    outgoing_latent = cache_latent[source_slot].reshape(
        (req_count, move_count) + cache_latent.shape[1:]
    )
    outgoing_rope = cache_rope[source_slot].reshape((req_count, move_count) + cache_rope.shape[1:])
    arrived = (
        lax.all_to_all(outgoing_latent, "req", split_axis=0, concat_axis=0, tiled=True),
        lax.all_to_all(outgoing_rope, "req", split_axis=0, concat_axis=0, tiled=True),
    )
    local_latent = arrived[0].reshape(cache_latent.shape)
    local_rope = arrived[1].reshape(cache_rope.shape)
    whole_latent, whole_rope = (
        lax.all_gather(local_latent, "exp", axis=1, tiled=True),
        lax.all_gather(local_rope, "exp", axis=1, tiled=True),
    )
    cache_keys = jnp.take_along_axis(whole_latent, page_table[:, :, None, None], axis=1).reshape(
        req_group, -1, whole_latent.shape[-1]
    )
    cache_rope_keys = jnp.take_along_axis(whole_rope, page_table[:, :, None], axis=1).reshape(
        req_group, -1, DR
    )
    normed = rms_scale(tokens, attn_gain).astype(jnp.bfloat16)
    angles = rope_angles(group_positions(cache_len, span_slot, SPAN), DR)
    query_nope = jnp.dot(normed, wq_nope, preferred_element_type=jnp.float32).astype(jnp.bfloat16)
    query_rope = rotate(
        jnp.dot(normed, wq_rope, preferred_element_type=jnp.float32).reshape(
            rows_group, heads_device, DR
        ),
        angles[:, None, :],
    ).astype(jnp.bfloat16)
    row_offset = lax.axis_index("exp") * rows_device
    own_normed = lax.dynamic_slice_in_dim(normed, row_offset, rows_device, 0)
    own_angles = lax.dynamic_slice_in_dim(angles, row_offset, rows_device, 0)
    own_latent = rms_scale(
        jnp.dot(own_normed, w_latent, preferred_element_type=jnp.float32), latent_gain
    ).astype(jnp.bfloat16)
    own_rope = rotate(
        jnp.dot(own_normed, w_krope, preferred_element_type=jnp.float32), own_angles
    ).astype(jnp.bfloat16)
    new_latent, new_rope = (
        lax.all_gather(own_latent, "exp", axis=0, tiled=True),
        lax.all_gather(own_rope, "exp", axis=0, tiled=True),
    )
    query_latent = dot_transposed(query_nope, w_uk).astype(jnp.bfloat16)
    attended = attend_head(
        query_latent,
        query_rope[:, 0],
        new_latent,
        new_rope,
        cache_keys,
        cache_rope_keys,
        cache_len,
        span_slot,
        SPAN,
        scale_factor,
    )
    head_outs = jnp.dot(attended, w_uv, preferred_element_type=jnp.float32).astype(jnp.bfloat16)
    attn_rows = lax.psum_scatter(
        jnp.dot(head_outs, w_out, preferred_element_type=jnp.float32).astype(jnp.bfloat16),
        "exp",
        scatter_dimension=0,
        tiled=True,
    ).astype(jnp.float32)
    own_tokens = lax.dynamic_slice_in_dim(tokens, row_offset, rows_device, 0)
    resid = (own_tokens.astype(jnp.float32) + attn_rows).astype(jnp.bfloat16)
    moe_in = rms_scale(resid, moe_gain).astype(jnp.bfloat16)
    picked = jnp.take_along_axis(
        jax.nn.sigmoid(jnp.dot(moe_in, w_router, preferred_element_type=jnp.float32)),
        routes,
        axis=1,
    )
    gate_w = route_scale * picked / jnp.sum(picked, axis=1, keepdims=True)
    expert_count = w_router.shape[1]
    capacity = 2 * ((rows_device * TOP // expert_count + 5) // 2)
    flat_routes = routes.reshape(-1)
    onehot = (flat_routes[:, None] == jnp.arange(expert_count, dtype=jnp.int32)[None, :]).astype(
        jnp.int32
    )
    slot_rank = jnp.sum((jnp.cumsum(onehot, axis=0) - 1) * onehot, axis=1)
    slot_of = flat_routes * capacity + slot_rank
    slot_index = jnp.arange(expert_count * capacity, dtype=jnp.int32)
    dispatch_rows = jnp.any(
        (slot_of[None, :] == slot_index[:, None]).reshape(
            expert_count * capacity, rows_device, TOP
        ),
        axis=2,
    ).astype(jnp.bfloat16)
    packed = jnp.dot(dispatch_rows, moe_in, preferred_element_type=jnp.float32).astype(jnp.bfloat16)
    halves_device = w_gate.shape[0]
    doubled = jnp.broadcast_to(
        packed.reshape(expert_count, 1, capacity, model_width),
        (expert_count, 2, capacity, model_width),
    ).reshape(device_count, halves_device, capacity, model_width)
    computed = expert_halves(
        lax.all_to_all(doubled, ("req", "exp"), split_axis=0, concat_axis=0, tiled=True),
        w_gate,
        w_up,
        w_down,
    )
    returned = lax.all_to_all(computed, ("req", "exp"), split_axis=0, concat_axis=0, tiled=True)
    paired = returned.reshape(expert_count, 2, capacity, model_width)
    expert_out = (
        (paired[:, 0].astype(jnp.float32) + paired[:, 1].astype(jnp.float32))
        .astype(jnp.bfloat16)
        .reshape(expert_count * capacity, model_width)
    )
    gathered = expert_out[slot_of].astype(jnp.float32).reshape(rows_device, TOP, model_width)
    moe_out = jnp.sum(gate_w[:, :, None] * gathered, axis=1)
    return (resid.astype(jnp.float32) + moe_out).astype(jnp.bfloat16)


def solution(mesh):
    in_specs = (
        P("req", None),
        P(),
        P(None, "exp"),
        P(None, "exp"),
        P(),
        P(),
        P(),
        P(None, "exp"),
        P(None, "exp"),
        P("exp", None),
        P(),
        P(),
        P(("req", "exp"), None, None),
        P(("req", "exp"), None, None),
        P(("req", "exp"), None, None),
        P(("req", "exp"), None),
        P("req", "exp", None, None),
        P("req", "exp", None),
        P("req"),
        P("req", None),
        P("req"),
        P("req"),
    )
    out_specs = P(("req", "exp"), None)
    return jax.shard_map(shards, mesh=mesh, in_specs=in_specs, out_specs=out_specs, check_vma=False)
```

profile of v0, /device:TPU:8, one launch (start us, length us, event | category | flops | bytes accessed | tf_op | source)
XLA Modules:
  0.0 632.7 jit_solution(2216624026873869297)
XLA Ops:
  6.5 0.8 convert_element_type.149
  7.4 3.1 fusion.1
  10.6 5.2 fusion.3
  15.9 2.3 multiply_reduce_fusion.1
  18.1 0.7 fusion.51
  20.5 9.7 %all_to_all.20 = bf16[8,2,1,2048]{3,1,2,0:T(2,128)(2,1)S(1)} all-to-all(bf16[8,2,1,2048]{3,1,2,0:T(2,128)(2,1)S(1)} %bitcast.125), channel_id=1, replica_groups=mesh['req'=8,'exp'=16] {'req'}, dimensions={0} | all-to-all | bytes 131072 | tf_op jit(solution)/shard_map/all_to_all | solution.py:182
  30.9 1.6 gather_fusion
  32.6 13.5 %all_to_all.21 = bf16[8,2,1,32,512]{4,3,1,2,0:T(8,128)(2,1)} all-to-all(bf16[8,2,1,32,512]{4,3,1,2,0:T(8,128)(2,1)S(1)} %bitcast.122), channel_id=1, replica_groups=mesh['req'=8,'exp'=16] {'req'}, dimensions={0} | all-to-all | bytes 1048576 | tf_op jit(solution)/shard_map/all_to_all | solution.py:181
  46.4 1.2 reduce-window.6
  50.6 1.4 fusion.29
  52.2 24.8 %all-gather.1 = bf16[16,65,64]{1,2,0:T(8,128)(2,1)S(1)} all-gather(bf16[1,65,64]{1,2,0:T(8,128)(2,1)S(1)} %maximum_bitcast_fusion), channel_id=1, replica_groups=mesh['req'=8,'exp'=16] {'exp'}, dimensions={0}, use_global_device_ids=true | all-gather | bytes 141440 | tf_op jit(solution)/shard_map/all_gather | solution.py:216
  77.4 3.7 convolution_bitcast_fusion
  81.9 0.7 iota_compare_fusion.7
  82.6 5.3 convolution_convert_fusion.3
  88.0 0.7 slice_bitcast_fusion.2
  88.7 2.4 reshape.471
  91.1 2.3 slice.94
  93.4 0.9 fusion.52
  94.2 14.4 %all-gather.8.cloned.1.call-done = bf16[16,16,2048]{2,0,1:T(8,128)(2,1)} async-done(((bf16[16,1,2048]{2,0,1:T(8,128)(2,1)}), bf16[16,16,2048]{2,0,1:T(8,128)(2,1)}) %all-gather.8.cloned.1.call-update) | async-done | bytes 1048592 | tf_op jit(solution)/shard_map/all_gather | solution.py:188
  108.6 2.8 copy.77
  111.4 5.1 gather_fusion.4
  116.6 4.4 gather.35
  121.0 3.2 broadcast_select_fusion
  124.2 1.4 copy-done.1
  125.7 2.2 fusion.87
  128.0 53.3 %all-gather.6.cloned.1.call-done = bf16[16,16,32,512]{3,2,0,1:T(8,128)(2,1)} async-done(((bf16[16,1,32,512]{3,2,0,1:T(8,128)(2,1)}), bf16[16,16,32,512]{3,2,0,1:T(8,128)(2,1)}) %all-gather.6.cloned.1.call-update) | async-done | bytes 8388624 | tf_op jit(solution)/shard_map/all_gather | solution.py:187
  181.3 13.4 %gather_fusion.3 = bf16[256,32,512]{2,1,0:T(8,128)(2,1)} fusion(bf16[16,16,32,512]{3,2,0,1:T(8,128)(2,1)} %all-gather.6.cloned.1.call-done, s32[256]{0:T(256)S(1)} %reshape.436), kind=kCustom, calls=%fused_computation.3 | custom fusion | bytes 16779264 | tf_op jit(solution)/shard_map/jit(take_along_axis)/gather | solution.py:190
  194.7 4.9 bitcast_select_fusion
  199.7 2.3 fusion.59
  202.5 1.2 fusion.57
  204.0 1.8 fusion.23
  205.8 2.3 fusion.86
  208.1 2.1 fusion.5
  210.2 3.4 fusion.12
  213.6 0.8 fusion.54
  214.4 5.1 convolution_convert_fusion.1
  219.6 66.6 %fusion = bf16[80,2048]{1,0:T(8,128)(2,1)S(1)} fusion(bf16[1040,2048]{1,0:T(8,128)(2,1)} %convolution_convert_fusion.1), kind=kCustom, calls=%all-reduce-scatter | all-reduce-scatter fusion | flops 2621441 | bytes 4588032
  286.2 0.8 slice.109
  287.0 3.4 collective-permute-start.1
  290.4 1.9 collective-permute-start
  292.3 3.9 collective-permute-start.2
  297.9 4.2 collective-permute-done.2
  302.2 6.0 collective-permute-done
  308.1 11.8 %concatenate.48 = bf16[305,2048]{1,0:T(8,128)(2,1)} concatenate(bf16[65,2048]{1,0:T(8,128)(2,1)} %collective-permute-done.2, bf16[80,2048]{1,0:T(8,128)(2,1)} %collective-permute-done.1, bf16[80,2048]{1,0:T(8,128)(2,1)} %collective-permute-done, bf16[80,2048]{1,0:T(8,128)(2,1)S(1)} %fusion), dimensions={0} | concatenate | bytes 2498560
  319.9 1.4 fusion.25
  321.3 2.5 convolution_convert_fusion.2
  323.7 5.4 broadcast_in_dim.120
  329.1 6.8 %broadcast_in_dim.121 = bf16[64,2,10,2048]{3,2,1,0:T(8,128)(2,1)} broadcast(bf16[64,10,2048]{2,1,0:T(8,128)(2,1)} %broadcast_in_dim.120), dimensions={0,2,3} | broadcast | bytes 7864320 | tf_op jit(solution)/shard_map/broadcast_in_dim | solution.py:264
  335.9 110.3 %all_to_all.22 = bf16[128,1,10,2048]{3,2,1,0:T(8,128)(2,1)} all-to-all(bf16[128,1,10,2048]{3,2,1,0:T(8,128)(2,1)} %bitcast.119), channel_id=1, replica_groups=mesh['req'=8,'exp'=16] {'req','exp'}, dimensions={0} | all-to-all | bytes 10485760 | tf_op jit(solution)/shard_map/all_to_all | solution.py:269
  446.2 9.8 %reshape_squeeze.3 = bf16[1280,2048]{1,0:T(8,128)(2,1)} reshape(bf16[128,1,10,2048]{3,2,1,0:T(8,128)(2,1)} %all_to_all.22) | data formatting | bytes 10485760 | tf_op jit(solution)/shard_map/reshape;squeeze | solution.py:132
  456.0 7.4 %fusion.10 = f32[1280,704]{0,1:T(8,128)S(1)} fusion(bf16[1280,2048]{1,0:T(8,128)(2,1)} %reshape_squeeze.3, bf16[1,2048,704]{1,2,0:T(8,128)(2,1)} %param.34), kind=kOutput, calls=%fused_computation.31 | convolution fusion | flops 3690987520 | bytes 11730944 | tf_op jit(solution)/shard_map/dot_general | solution.py:124
  463.5 4.2 fusion.6
  467.7 6.1 convolution_convert_fusion
  473.8 9.5 %stack_reshape.3 = bf16[128,1,10,2048]{3,2,0,1:T(8,128)(2,1)} reshape(bf16[1280,2048]{1,0:T(8,128)(2,1)} %convolution_convert_fusion) | data formatting | bytes 10485760 | tf_op jit(solution)/shard_map/stack;reshape | solution.py:135
  483.3 6.1 all-to-all-start.3
  489.9 1.3 fusion.15
  491.2 4.8 gather_fusion.5
  496.3 102.8 %all-to-all-done.3 = bf16[128,1,10,2048]{3,2,1,0:T(8,128)(2,1)} async-done(((bf16[128,1,10,2048]{3,2,1,0:T(8,128)(2,1)}), bf16[128,1,10,2048]{3,2,1,0:T(8,128)(2,1)}, u32[]{:S(2)}, u32[]{:S(2)}) %all-to-all-start.3) | async-done | bytes 5242912 | tf_op jit(solution)/shard_map/all_to_all | solution.py:274
  599.1 5.7 add_convert_fusion
  604.8 5.5 convert_element_type.181
  610.3 7.2 %gather_fusion.2 = bf16[390,2048]{1,0:T(8,128)(2,1)} fusion(bf16[640,2048]{1,0:T(8,128)(2,1)} %convert_element_type.181, s32[1024]{0:T(1024)S(1)} %pad_clamp_fusion), kind=kCustom, calls=%fused_computation.2 | custom fusion | bytes 3196440 | tf_op jit(solution)/shard_map/gather | solution.py:281
  617.5 3.9 reshape.400
  621.4 3.8 multiply_reduce_fusion
  625.2 0.8 fusion.28
  (105 shorter events, 8.3 us)
Async XLA Ops:
  6.5 461.2 %copy-start = (bf16[1,704,2048]{2,1,0:T(8,128)(2,1)S(1)}, bf16[1,704,2048]{2,1,0:T(8,128)(2,1)}, u32[]{:S(2)}) copy-start(bf16[1,704,2048]{2,1,0:T(8,128)(2,1)} %param.36) | copy-start | bytes 8650756
  6.5 4.0 copy-start.12
  6.5 82.1 %all-gather.10.cloned.1.call-start = ((), (), s32[]{:S(2)}) async-start(), calls=%async_computation.6 | async-start | bytes 1253376 | tf_op jit(solution)/shard_map/all_gather | solution.py:215
  10.6 8.4 %copy-start.15 = (s32[16]{0:T(128)S(1)}, s32[16]{0:T(128)}, u32[]{:S(2)}) copy-start(s32[16]{0:T(128)} %param.40) | copy-start | bytes 196
  10.6 9.2 %copy-start.3 = (bf16[16,1,2048]{2,0,1:T(8,128)(2,1)S(1)}, bf16[16,1,2048]{2,0,1:T(8,128)(2,1)}, u32[]{:S(2)}) copy-start(bf16[16,1,2048]{2,0,1:T(8,128)(2,1)} %param.39) | copy-start | bytes 196612
  15.8 30.2 %copy-start.8 = (s32[65,6]{0,1:T(8,128)S(1)}, s32[65,6]{0,1:T(8,128)}, u32[]{:S(2)}) copy-start(s32[65,6]{0,1:T(8,128)} %param.37) | copy-start | bytes 4684
  15.9 32.3 %copy-start.9 = (s32[16,16]{1,0:T(8,128)S(1)}, s32[16,16]{1,0:T(8,128)}, u32[]{:S(2)}) copy-start(s32[16,16]{1,0:T(8,128)} %param.41) | copy-start | bytes 3076
  15.9 33.3 %copy-start.10 = (s32[16]{0:T(128)S(1)}, s32[16]{0:T(128)}, u32[]{:S(2)}) copy-start(s32[16]{0:T(128)} %param.42) | copy-start | bytes 196
  18.9 89.7 %all-gather.8.cloned.1.call-start = ((), (), s32[]{:S(2)}) async-start(), calls=%async_computation.5 | async-start | bytes 1114112 | tf_op jit(solution)/shard_map/all_gather | solution.py:188
  30.9 150.4 %all-gather.6.cloned.1.call-start = ((), (), s32[]{:S(2)}) async-start(), calls=%async_computation.4 | async-start | bytes 8912896 | tf_op jit(solution)/shard_map/all_gather | solution.py:187
  77.4 10.5 %copy-start.6 = (bf16[1040,64]{0,1:T(8,128)(2,1)}, bf16[1040,64]{0,1:T(8,128)(2,1)S(1)}, u32[]{:S(2)}) copy-start(bf16[1040,64]{0,1:T(8,128)(2,1)S(1)} %reshape.473) | copy-start | bytes 399364
  124.2 1.4 copy-start.1
  202.4 1.2 copy-start.4
  202.4 1.5 copy-start.5
  204.0 1.8 slice-start
  210.2 4.2 copy-start.7
  214.4 81.9 %copy-start.11 = (bf16[2048]{0:T(1024)(128)(2,1)S(1)}, bf16[2048]{0:T(1024)(128)(2,1)}, u32[]{:S(2)}) copy-start(bf16[2048]{0:T(1024)(128)(2,1)} %param.32) | copy-start | bytes 12292
  214.4 81.9 %copy-start.13 = (u32[128]{0:T(128)S(1)}, u32[128]{0:T(128)}, u32[]{:S(2)}) copy-start(u32[128]{0:T(128)} %constant.195) | copy-start | bytes 1540
  287.0 15.2 %collective-permute-start.1 = (bf16[80,2048]{1,0:T(8,128)(2,1)S(1)}, bf16[80,2048]{1,0:T(8,128)(2,1)}, u32[]{:S(2)}, u32[]{:S(2)}) collective-permute-start(bf16[80,2048]{1,0:T(8,128)(2,1)S(1)} %fusion), channel_id=1, source_target_pairs={{0,2},{1,3},{2,4},{3,5},{4,6},{5,7},{6,8},{7,9},{8,10},{9,11},{10,... | collective-permute-start | bytes 983048
  290.4 17.7 %collective-permute-start = (bf16[80,2048]{1,0:T(8,128)(2,1)S(1)}, bf16[80,2048]{1,0:T(8,128)(2,1)}, u32[]{:S(2)}, u32[]{:S(2)}) collective-permute-start(bf16[80,2048]{1,0:T(8,128)(2,1)S(1)} %fusion), channel_id=1, source_target_pairs={{0,1},{1,2},{2,3},{3,4},{4,5},{5,6},{6,7},{7,8},{8,9},{9,10},{10,1... | collective-permute-start | bytes 983048
  292.3 9.8 %collective-permute-start.2 = (bf16[65,2048]{1,0:T(8,128)(2,1)}, bf16[65,2048]{1,0:T(8,128)(2,1)}, u32[]{:S(2)}, u32[]{:S(2)}) collective-permute-start(bf16[65,2048]{1,0:T(8,128)(2,1)} %slice.109), channel_id=1, source_target_pairs={{0,3},{1,4},{2,5},{3,6},{4,7},{5,8},{6,9},{7,10},{8,11},{9,12},{10... | collective-permute-start | bytes 798728
  456.0 7.5 %copy-start.2 = (bf16[1280,2048]{1,0:T(8,128)(2,1)S(1)}, bf16[1280,2048]{1,0:T(8,128)(2,1)}, u32[]{:S(2)}) copy-start(bf16[1280,2048]{1,0:T(8,128)(2,1)} %reshape_squeeze.3) | copy-start | bytes 15728644
  456.0 7.5 %copy-start.14 = (bf16[1,2048,704]{1,2,0:T(8,128)(2,1)S(1)}, bf16[1,2048,704]{1,2,0:T(8,128)(2,1)}, u32[]{:S(2)}) copy-start(bf16[1,2048,704]{1,2,0:T(8,128)(2,1)} %param.35) | copy-start | bytes 8650756
  483.3 115.7 %all-to-all-start.3 = ((bf16[128,1,10,2048]{3,2,1,0:T(8,128)(2,1)}), bf16[128,1,10,2048]{3,2,1,0:T(8,128)(2,1)}, u32[]{:S(2)}, u32[]{:S(2)}) async-start(bf16[128,1,10,2048]{3,2,1,0:T(8,128)(2,1)} %bitcast.117), calls=%async_computation.3 | async-start | bytes 16777216 | tf_op jit(solution)/shard_map/all_to_all | solution.py:274
Sparse Core Ops, SparseCore 0:
  19.0 45.2 all-gather.9
  66.4 42.1 all-gather.7
  110.8 70.4 all-gather.5
where the time goes:
time: 641 us; the launch traced here: 633 us
  blocking collectives  225 us (35%)
  waiting for transfers between devices  181 us (28%)
  local copies, waits for them, and re-layouts  105 us (16%)
  matrix products  52.5 us (8%)
  other arithmetic  38.1 us (6%)
  between operations  15.9 us (2%)
  starting transfers between devices  15.5 us (2%)
    all_to_all x1, blocking collectives, shards(): lax.all_to_all(doubled, ('req', 'exp'), split_axis=0, concat_axis=0, tile...  110 us
    all_to_all x1, waiting for transfers between devices, shards(): lax.all_to_all(computed, ('req', 'exp'), split_axis=0, concat_axis=0, til...  103 us
    unnamed x1, blocking collectives  66.6 us
    all_gather x1, waiting for transfers between devices, shards(): lax.all_gather(local_latent, 'exp', axis=1, tiled=True)  53.3 us
    all_gather x1, blocking collectives, shards(): lax.all_gather(own_rope, 'exp', axis=0, tiled=True)  24.8 us
    unnamed x38, local copies, waits for them, and re-layouts  17.8 us
    all_gather x1, waiting for transfers between devices, shards(): lax.all_gather(local_rope, 'exp', axis=1, tiled=True)  14.4 us
    gather x2, local copies, waits for them, and re-layouts, shards(): jnp.take_along_axis(whole_latent, page_table[:, :, None, None], axis=1)  13.5 us
  transfers between devices with their start and end apart: 7, of which 5 were waited for; matrix products, arithmetic and copies ran while one was open for 8% of the time, Pallas kernels for 0%

commit v1 on v0

--- a/solution.py
+++ b/solution.py
@@ -183,8 +183,16 @@
     )
     local_latent = arrived[0].reshape(cache_latent.shape)
     local_rope = arrived[1].reshape(cache_rope.shape)
+
+    def group_set(buf):
+        far_arr = jnp.concatenate(
+            jax.lax.all_to_all(jnp.stack(jax.lax.psum(1, "exp") * [buf], axis=0), "exp", 0, 0),
+            axis=1,
+        )
+        return far_arr
+
     whole_latent, whole_rope = (
-        lax.all_gather(local_latent, "exp", axis=1, tiled=True),
+        group_set(local_latent),
         lax.all_gather(local_rope, "exp", axis=1, tiled=True),
     )
     cache_keys = jnp.take_along_axis(whole_latent, page_table[:, :, None, None], axis=1).reshape(

time: 641 us -> 725 us (1.13)
  blocking collectives: 225 us -> 331 us
  waiting for transfers between devices: 181 us -> 137 us
  starting transfers between devices: 15.5 us -> 28.3 us
  local copies, waits for them, and re-layouts: 105 us -> 115 us
    all_gather x1, blocking collectives: 24.8 us -> 141 us  [shards(): lax.all_gather(own_rope, 'exp', axis=0, tiled=True)]
    all_gather x1 -> x0, waiting for transfers between devices: 53.3 us -> none  [shards(): lax.all_gather(local_latent, 'exp', axis=1, tiled=True)]
    all_to_all x0 -> x2, starting transfers between devices: none -> 12.8 us  [the longest x1 8.54 us: group_set(): jax.lax.all_to_all(jnp.stack(jax.lax.psum(1, 'exp') * [buf], axis=0), 'ex...]
    all_to_all x1 -> x0, blocking collectives: 9.72 us -> none  [shards(): lax.all_to_all(outgoing_rope, 'req', split_axis=0, concat_axis=0, tiled=T...]
    unnamed x38 -> x56, local copies, waits for them, and re-layouts: 17.8 us -> 20.7 us
  transfers between devices with their start and end apart: 7 -> 8, of which waited for: 5 -> 5; matrix products, arithmetic and copies ran while one was open for 8% -> 8% of each run, Pallas kernels for 0% -> 0%
where the time goes in v1:
time: 725 us; the launch traced here: 716 us
  blocking collectives  331 us (46%)
  waiting for transfers between devices  137 us (19%)
  local copies, waits for them, and re-layouts  115 us (16%)
  matrix products  50.6 us (7%)
  other arithmetic  38.1 us (5%)
  starting transfers between devices  28.3 us (4%)
  between operations  16.2 us (2%)
    all_gather x1, blocking collectives, shards(): lax.all_gather(own_rope, 'exp', axis=0, tiled=True)  141 us
    all_to_all x1, blocking collectives, shards(): lax.all_to_all(doubled, ('req', 'exp'), split_axis=0, concat_axis=0, tile...  110 us
    all_to_all x1, waiting for transfers between devices, shards(): lax.all_to_all(computed, ('req', 'exp'), split_axis=0, concat_axis=0, til...  103 us
    unnamed x1, blocking collectives  66.5 us
    unnamed x56, local copies, waits for them, and re-layouts  20.7 us
    all_gather x1, waiting for transfers between devices, shards(): lax.all_gather(local_rope, 'exp', axis=1, tiled=True)  20 us
  transfers between devices with their start and end apart: 8, of which 5 were waited for; matrix products, arithmetic and copies ran while one was open for 8% of the time, Pallas kernels for 0%

profile of v1, /device:TPU:8, one launch (start us, length us, event | category | flops | bytes accessed | tf_op | source)
XLA Modules:
  0.0 715.8 jit_solution(6303297692687082032)
XLA Ops:
  6.5 1.0 convert_reduce_fusion
  8.8 1.5 gather_fusion.1
  11.0 4.3 all-to-all-start.2
  15.3 1.6 gather_fusion
  17.0 4.0 all-to-all-done.2
  21.0 12.8 %all_to_all.25 = bf16[8,2,1,32,512]{4,3,1,2,0:T(8,128)(2,1)S(1)} all-to-all(bf16[8,2,1,32,512]{4,3,1,2,0:T(8,128)(2,1)S(1)} %bitcast.125), channel_id=1, replica_groups=mesh['req'=8,'exp'=16] {'req'}, dimensions={0} | all-to-all | bytes 1048576 | tf_op jit(solution)/shard_map/all_to_all | solution.py:181
  33.8 4.3 stack.3
  38.0 8.5 %all-to-all-start.1 = ((bf16[16,16,1,32,512]{4,3,2,1,0:T(8,128)(2,1)}), bf16[16,16,1,32,512]{4,3,2,1,0:T(8,128)(2,1)}, u32[]{:S(2)}, u32[]{:S(2)}) async-start(bf16[16,16,1,32,512]{4,3,2,1,0:T(8,128)(2,1)} %stack.3), calls=%async_computation.1 | async-start | bytes 16777216 | tf_op jit(solution)/shard_map/all_to_all | solution.py:189
  46.7 3.1 fusion.1
  49.8 3.4 fusion.3
  53.2 2.0 copy-done.1
  56.9 1.2 reduce-window.6
  60.8 1.4 fusion.85
  64.1 1.2 fusion.29
  66.2 141.5 %all-gather.1 = bf16[16,65,64]{1,2,0:T(8,128)(2,1)S(1)} all-gather(bf16[1,65,64]{1,2,0:T(8,128)(2,1)S(1)} %maximum_bitcast_fusion), channel_id=1, replica_groups=mesh['req'=8,'exp'=16] {'exp'}, dimensions={0}, use_global_device_ids=true | all-gather | bytes 141440 | tf_op jit(solution)/shard_map/all_gather | solution.py:224
  208.2 3.7 convolution_bitcast_fusion
  213.3 5.3 convolution_convert_fusion.3
  219.3 2.4 reshape.479
  221.7 2.3 slice.94
  224.0 0.9 fusion.52
  224.9 20.0 %all-gather.5.cloned.1.call-done = bf16[16,16,2048]{2,0,1:T(8,128)(2,1)} async-done(((bf16[16,1,2048]{2,0,1:T(8,128)(2,1)}), bf16[16,16,2048]{2,0,1:T(8,128)(2,1)}) %all-gather.5.cloned.1.call-update) | async-done | bytes 1048592 | tf_op jit(solution)/shard_map/all_gather | solution.py:196
  244.9 2.8 copy.77
  247.6 5.2 gather_fusion.4
  252.8 4.4 gather.35
  257.2 3.2 broadcast_select_fusion
  260.5 1.3 copy-done.2
  261.9 2.2 fusion.87
  264.1 13.5 %gather_fusion.3 = bf16[256,32,512]{2,1,0:T(8,128)(2,1)} fusion(bf16[16,16,32,512]{3,2,0,1:T(8,128)(2,1)} %bitcast.6, s32[256]{0:T(256)S(1)} %reshape.444), kind=kCustom, calls=%fused_computation.3 | custom fusion | bytes 16779264 | tf_op jit(solution)/shard_map/jit(take_along_axis)/gather | solution.py:198
  277.6 4.9 bitcast_select_fusion
  282.6 2.3 fusion.59
  285.4 1.2 fusion.57
  286.9 1.8 fusion.23
  288.7 2.3 fusion.86
  291.0 2.1 fusion.5
  293.1 3.4 fusion.12
  296.6 0.8 fusion.54
  297.4 5.1 convolution_convert_fusion.1
  302.5 66.5 %fusion = bf16[80,2048]{1,0:T(8,128)(2,1)S(1)} fusion(bf16[1040,2048]{1,0:T(8,128)(2,1)} %convolution_convert_fusion.1), kind=kCustom, calls=%all-reduce-scatter | all-reduce-scatter fusion | flops 2621441 | bytes 4588032
  369.8 3.4 collective-permute-start.1
  373.2 1.9 collective-permute-start
  375.2 3.9 collective-permute-start.2
  380.8 4.2 collective-permute-done.2
  385.0 6.0 collective-permute-done
  391.0 11.8 %concatenate.48 = bf16[305,2048]{1,0:T(8,128)(2,1)} concatenate(bf16[65,2048]{1,0:T(8,128)(2,1)} %collective-permute-done.2, bf16[80,2048]{1,0:T(8,128)(2,1)} %collective-permute-done.1, bf16[80,2048]{1,0:T(8,128)(2,1)} %collective-permute-done, bf16[80,2048]{1,0:T(8,128)(2,1)S(1)} %fusion), dimensions={0} | concatenate | bytes 2498560
  402.8 1.4 fusion.25
  404.1 2.5 convolution_convert_fusion.2
  406.6 5.4 broadcast_in_dim.120
  412.0 6.8 broadcast_in_dim.121
  418.7 110.3 %all_to_all.26 = bf16[128,1,10,2048]{3,2,1,0:T(8,128)(2,1)} all-to-all(bf16[128,1,10,2048]{3,2,1,0:T(8,128)(2,1)} %bitcast.122), channel_id=1, replica_groups=mesh['req'=8,'exp'=16] {'req','exp'}, dimensions={0} | all-to-all | bytes 10485760 | tf_op jit(solution)/shard_map/all_to_all | solution.py:277
  529.0 9.8 %reshape_squeeze.3 = bf16[1280,2048]{1,0:T(8,128)(2,1)} reshape(bf16[128,1,10,2048]{3,2,1,0:T(8,128)(2,1)} %all_to_all.26) | data formatting | bytes 10485760 | tf_op jit(solution)/shard_map/reshape;squeeze | solution.py:132
  538.9 7.4 %fusion.10 = f32[1280,704]{0,1:T(8,128)S(1)} fusion(bf16[1280,2048]{1,0:T(8,128)(2,1)} %reshape_squeeze.3, bf16[1,2048,704]{1,2,0:T(8,128)(2,1)} %param.34), kind=kOutput, calls=%fused_computation.31 | convolution fusion | flops 3690987520 | bytes 11730944 | tf_op jit(solution)/shard_map/dot_general | solution.py:124
  546.4 4.2 fusion.6
  550.6 6.1 convolution_convert_fusion
  556.7 9.5 %stack_reshape.5 = bf16[128,1,10,2048]{3,2,0,1:T(8,128)(2,1)} reshape(bf16[1280,2048]{1,0:T(8,128)(2,1)} %convolution_convert_fusion) | data formatting | bytes 10485760 | tf_op jit(solution)/shard_map/stack;reshape | solution.py:135
  566.2 6.1 all-to-all-start.4
  572.8 1.3 fusion.15
  574.1 4.8 gather_fusion.5
  579.2 102.7 %all-to-all-done.4 = bf16[128,1,10,2048]{3,2,1,0:T(8,128)(2,1)} async-done(((bf16[128,1,10,2048]{3,2,1,0:T(8,128)(2,1)}), bf16[128,1,10,2048]{3,2,1,0:T(8,128)(2,1)}, u32[]{:S(2)}, u32[]{:S(2)}) %all-to-all-start.4) | async-done | bytes 5242912 | tf_op jit(solution)/shard_map/all_to_all | solution.py:282
  681.9 5.7 add_convert_fusion
  687.6 5.5 convert_element_type.181
  693.2 7.2 gather_fusion.2
  700.3 3.9 reshape.408
  704.2 3.8 multiply_reduce_fusion
  708.0 0.8 fusion.28
  (124 shorter events, 13.9 us)
Async XLA Ops:
  6.5 544.0 %copy-start = (bf16[1,704,2048]{2,1,0:T(8,128)(2,1)S(1)}, bf16[1,704,2048]{2,1,0:T(8,128)(2,1)}, u32[]{:S(2)}) copy-start(bf16[1,704,2048]{2,1,0:T(8,128)(2,1)} %param.36) | copy-start | bytes 8650756
  11.0 9.9 %all-to-all-start.2 = ((bf16[8,2,1,2048]{3,1,2,0:T(2,128)(2,1)}), bf16[8,2,1,2048]{3,1,2,0:T(2,128)(2,1)S(1)}, u32[]{:S(2)}, u32[]{:S(2)}) async-start(bf16[8,2,1,2048]{3,1,2,0:T(2,128)(2,1)} %bitcast.16), calls=%async_computation.2 | async-start | bytes 131072 | tf_op jit(solution)/shard_map/all_to_all | solution.py:182
  38.0 8.6 %copy-start.18 = (bf16[2048]{0:T(1024)(128)(2,1)S(1)}, bf16[2048]{0:T(1024)(128)(2,1)}, u32[]{:S(2)}) copy-start(bf16[2048]{0:T(1024)(128)(2,1)} %param.23) | copy-start | bytes 12292
  38.0 8.6 %copy-start.22 = (bf16[512]{0:T(512)(128)(2,1)S(1)}, bf16[512]{0:T(512)(128)(2,1)}, u32[]{:S(2)}) copy-start(bf16[512]{0:T(512)(128)(2,1)} %param.28) | copy-start | bytes 3076
  38.0 226.1 %all-to-all-start.1 = ((bf16[16,16,1,32,512]{4,3,2,1,0:T(8,128)(2,1)}), bf16[16,16,1,32,512]{4,3,2,1,0:T(8,128)(2,1)}, u32[]{:S(2)}, u32[]{:S(2)}) async-start(bf16[16,16,1,32,512]{4,3,2,1,0:T(8,128)(2,1)} %stack.3), calls=%async_computation.1 | async-start | bytes 16777216 | tf_op jit(solution)/shard_map/all_to_all | solution.py:189
  46.6 172.8 %all-gather.7.cloned.1.call-start = ((), (), s32[]{:S(2)}) async-start(), calls=%async_computation.6 | async-start | bytes 1253376 | tf_op jit(solution)/shard_map/all_gather | solution.py:223
  49.8 5.4 copy-start.4
  49.8 6.8 copy-start.10
  49.8 9.3 %copy-start.14 = (s32[16,16]{1,0:T(8,128)S(1)}, s32[16,16]{1,0:T(8,128)}, u32[]{:S(2)}) copy-start(s32[16,16]{1,0:T(8,128)} %param.41) | copy-start | bytes 3076
  53.2 2.0 copy-start.1
  55.2 8.9 %copy-start.9 = (bf16[2048,64]{0,1:T(8,128)(2,1)S(1)}, bf16[2048,64]{0,1:T(8,128)(2,1)}, u32[]{:S(2)}) copy-start(bf16[2048,64]{0,1:T(8,128)(2,1)} %param.27) | copy-start | bytes 786436
  56.5 188.4 %all-gather.5.cloned.1.call-start = ((), (), s32[]{:S(2)}) async-start(), calls=%async_computation.5 | async-start | bytes 1114112 | tf_op jit(solution)/shard_map/all_gather | solution.py:196
  58.5 0.6 copy-start.16
  63.5 0.6 copy-start.12
  64.1 2.1 copy-start.20
  65.4 146.5 %copy-start.13 = (f32[1040]{0:T(1024)S(1)}, f32[1040]{0:T(1024)}, u32[]{:S(2)}) copy-start(f32[1040]{0:T(1024)} %copy-done.12) | copy-start | bytes 12484
  207.7 4.2 copy-start.21
  208.1 10.5 %copy-start.7 = (bf16[1040,64]{0,1:T(8,128)(2,1)}, bf16[1040,64]{0,1:T(8,128)(2,1)S(1)}, u32[]{:S(2)}) copy-start(bf16[1040,64]{0,1:T(8,128)(2,1)S(1)} %reshape.481) | copy-start | bytes 399364
  260.4 1.4 copy-start.2
  282.6 2.3 copy-start.15
  285.4 1.2 copy-start.5
  285.4 1.5 copy-start.6
  286.9 1.8 slice-start
  293.1 4.2 copy-start.8
  297.3 81.8 %copy-start.19 = (bf16[2048]{0:T(1024)(128)(2,1)S(1)}, bf16[2048]{0:T(1024)(128)(2,1)}, u32[]{:S(2)}) copy-start(bf16[2048]{0:T(1024)(128)(2,1)} %param.32) | copy-start | bytes 12292
  297.4 81.8 %copy-start.23 = (u32[128]{0:T(128)S(1)}, u32[128]{0:T(128)}, u32[]{:S(2)}) copy-start(u32[128]{0:T(128)} %constant.195) | copy-start | bytes 1540
  369.8 15.2 %collective-permute-start.1 = (bf16[80,2048]{1,0:T(8,128)(2,1)S(1)}, bf16[80,2048]{1,0:T(8,128)(2,1)}, u32[]{:S(2)}, u32[]{:S(2)}) collective-permute-start(bf16[80,2048]{1,0:T(8,128)(2,1)S(1)} %fusion), channel_id=1, source_target_pairs={{0,2},{1,3},{2,4},{3,5},{4,6},{5,7},{6,8},{7,9},{8,10},{9,11},{10,... | collective-permute-start | bytes 983048
  373.2 17.7 %collective-permute-start = (bf16[80,2048]{1,0:T(8,128)(2,1)S(1)}, bf16[80,2048]{1,0:T(8,128)(2,1)}, u32[]{:S(2)}, u32[]{:S(2)}) collective-permute-start(bf16[80,2048]{1,0:T(8,128)(2,1)S(1)} %fusion), channel_id=1, source_target_pairs={{0,1},{1,2},{2,3},{3,4},{4,5},{5,6},{6,7},{7,8},{8,9},{9,10},{10,1... | collective-permute-start | bytes 983048
  375.2 9.8 %collective-permute-start.2 = (bf16[65,2048]{1,0:T(8,128)(2,1)}, bf16[65,2048]{1,0:T(8,128)(2,1)}, u32[]{:S(2)}, u32[]{:S(2)}) collective-permute-start(bf16[65,2048]{1,0:T(8,128)(2,1)} %slice.109), channel_id=1, source_target_pairs={{0,3},{1,4},{2,5},{3,6},{4,7},{5,8},{6,9},{7,10},{8,11},{9,12},{10... | collective-permute-start | bytes 798728
  538.9 7.4 %copy-start.3 = (bf16[1280,2048]{1,0:T(8,128)(2,1)S(1)}, bf16[1280,2048]{1,0:T(8,128)(2,1)}, u32[]{:S(2)}) copy-start(bf16[1280,2048]{1,0:T(8,128)(2,1)} %reshape_squeeze.3) | copy-start | bytes 15728644
  538.9 7.5 %copy-start.24 = (bf16[1,2048,704]{1,2,0:T(8,128)(2,1)S(1)}, bf16[1,2048,704]{1,2,0:T(8,128)(2,1)}, u32[]{:S(2)}) copy-start(bf16[1,2048,704]{1,2,0:T(8,128)(2,1)} %param.35) | copy-start | bytes 8650756
  566.2 6.3 copy-start.11
  566.2 6.6 copy-start.17
  566.2 115.7 %all-to-all-start.4 = ((bf16[128,1,10,2048]{3,2,1,0:T(8,128)(2,1)}), bf16[128,1,10,2048]{3,2,1,0:T(8,128)(2,1)}, u32[]{:S(2)}, u32[]{:S(2)}) async-start(bf16[128,1,10,2048]{3,2,1,0:T(8,128)(2,1)} %bitcast.120), calls=%async_computation.4 | async-start | bytes 16777216 | tf_op jit(solution)/shard_map/all_to_all | solution.py:282
Sparse Core Ops, SparseCore 0:
  56.6 125.9 all-gather.6
  184.8 60.0 all-gather.4
